TPU v7x, 256 devices: a whole 4x4x8 slice. The times are simulated.
256 devices in a mesh: fsdp: 32 (over z, y_hi, core), tp: 8 (over y_lo, x).
Axes of the slice: x: 4, y: 4 (y_hi: 2, y_lo: 2; y = y_hi * 2 + y_lo), z: 8, core: 2. Of those that a mesh axis runs over, the one named last changes fastest.
Arguments:
- train_x: bfloat16 [32768, 8192], P('fsdp'), may hold values from -6 to 6
- train_q: bfloat16 [32768, 8192], P('fsdp', 'tp'), may hold values from -17 to 17
- train_k: bfloat16 [32768, 1024], P('fsdp', 'tp'), may hold values from -14 to 14
- train_target: bfloat16 [32768, 8192], P('fsdp', 'tp'), may hold values from -6 to 6
- train_skill: int32 [128], replicated, may hold values from 0 to 3, as said below
- value_weight: bfloat16 [8192, 1024], P('fsdp', 'tp'), may hold values from -0.0625 to 0.0625
- val_x: bfloat16 [4096, 8192], P('fsdp'), may hold values from -6 to 6
- val_q: bfloat16 [4096, 8192], P('fsdp', 'tp'), may hold values from -17 to 17
- val_k: bfloat16 [4096, 1024], P('fsdp', 'tp'), may hold values from -14 to 14
- val_target: bfloat16 [4096, 8192], P('fsdp', 'tp'), may hold values from -6 to 6
- val_skill: int32 [32], replicated, may hold values from 0 to 3, as said below
Outputs:
- skill_grads: bfloat16 [4, 8192, 1024], P(None, 'fsdp', 'tp')
- transfer: float32 [4, 4], replicated
Inputs may be any that keep to these rules, and one draw needn't show every extreme that they name: `train_skill`: each of the 4 skills labels exactly 32 sequences. `val_skill`: each of the 4 skills labels exactly 8 sequences.
All inputs are finite; a program needn't handle non-finite values.
Results may differ from a plain program's by a relative error of at most 0.0052.
The roundings to bfloat16 on the way count: a program that leaves them out, or rounds other values in their place, can miss the bound.
Values may be sent and summed in bfloat16 or wider, within the bound.
No kernel may reach another device: no remote copies, remote signals or barrier semaphores. Data moves between devices by JAX's collectives and lax.ppermute only.
A program may use at most 192 MiB of HBM per device.

v0:
```python
import math
import jax
import jax.numpy as jnp
from jax import lax
from jax.sharding import PartitionSpec as P

HD = 128
SKILLS = 4
SEQ = 256
VSEQ = 128
step_size = 0.01


def attend(query_rows, key_rows, length):
    members = query_rows.shape[0] // length
    kv_heads = key_rows.shape[1] // HD
    group = query_rows.shape[1] // HD // kv_heads
    queries = query_rows.reshape(members, length, kv_heads, group, HD)
    keys = key_rows.reshape(members, length, kv_heads, HD)
    scores = jnp.einsum("bqgrh,bkgh->bgrqk", queries, keys, preferred_element_type=jnp.float32) * (
        1.0 / math.sqrt(HD)
    )
    places = jnp.arange(length)
    allowed = places[:, None] >= places[None, :]
    scores = jnp.where(allowed, scores, jnp.float32(-1e30))
    highest = jnp.max(scores, axis=-1, keepdims=True)
    raised = jnp.exp(scores - highest)
    return (raised / jnp.sum(raised, axis=-1, keepdims=True)).astype(jnp.bfloat16)


def on_device(
    train_x,
    train_q,
    train_k,
    train_target,
    train_skill,
    value_weight,
    val_x,
    val_q,
    val_k,
    val_target,
    val_skill,
):
    head_width = train_k.shape[1]
    kv_heads = head_width // HD
    group = train_q.shape[1] // head_width
    train_rows = train_x.shape[0]
    val_rows = val_x.shape[0]
    train_members = train_rows // SEQ
    val_members = val_rows // VSEQ
    skill_ids = jnp.arange(SKILLS, dtype=jnp.int32)
    shard_rows = lax.all_gather(value_weight, "fsdp", axis=0, tiled=True)
    values = jnp.dot(train_x, shard_rows, preferred_element_type=jnp.float32)
    val_values = jnp.dot(val_x, shard_rows, preferred_element_type=jnp.float32)
    values = values.astype(jnp.bfloat16)
    val_values = val_values.astype(jnp.bfloat16)
    attention = attend(train_q, train_k, SEQ)
    value_blocks = values.reshape(train_members, SEQ, kv_heads, HD)
    mixed = jnp.einsum(
        "bgrqk,bkgh->bqgrh", attention, value_blocks, preferred_element_type=jnp.float32
    )
    target_blocks = train_target.reshape(train_members, SEQ, kv_heads, group, HD).astype(
        jnp.float32
    )
    residual = ((mixed - target_blocks) / SEQ).astype(jnp.bfloat16)
    value_grads = jnp.einsum(
        "bgrqk,bqgrh->bkgh", attention, residual, preferred_element_type=jnp.float32
    )
    grad_rows = value_grads.reshape(train_rows, head_width).astype(jnp.bfloat16)
    train_first = lax.axis_index("fsdp") * train_members
    local_skill = lax.dynamic_slice_in_dim(train_skill, train_first, train_members)
    local_indicator = (local_skill[:, None] == skill_ids[None, :]).astype(jnp.float32)
    running = jnp.zeros(
        (lax.axis_size("fsdp") * (train_x.shape[1] // lax.axis_size("fsdp")), SKILLS, head_width),
        jnp.float32,
    )
    for sequence in range(train_members):
        product = jnp.dot(
            train_x[sequence * SEQ : (sequence + 1) * SEQ].T,
            grad_rows[sequence * SEQ : (sequence + 1) * SEQ],
            preferred_element_type=jnp.float32,
        )
        running = running + local_indicator[sequence][None, :, None] * product[:, None, :]
    shares = lax.psum_scatter(running, "fsdp", scatter_dimension=0, tiled=True)
    skill_grads = jnp.transpose(shares, (1, 0, 2)).astype(jnp.bfloat16)
    val_attention = attend(val_q, val_k, VSEQ)
    val_blocks = val_values.reshape(val_members, VSEQ, kv_heads, HD)
    val_mixed = jnp.einsum(
        "bgrqk,bkgh->bqgrh", val_attention, val_blocks, preferred_element_type=jnp.float32
    )
    val_target_blocks = val_target.reshape(val_members, VSEQ, kv_heads, group, HD).astype(
        jnp.float32
    )
    val_residual = (val_mixed - val_target_blocks) / VSEQ
    val_pull = jnp.einsum(
        "bgrqk,bqgrh->bkgh",
        val_attention.astype(jnp.float32),
        val_residual,
        precision=lax.Precision.HIGHEST,
    )
    val_pull = val_pull.reshape(val_rows, head_width)
    tangent = jnp.einsum(
        "td,sdc->tsc",
        val_x,
        lax.all_gather(skill_grads, "fsdp", axis=1, tiled=True),
        preferred_element_type=jnp.float32,
    )
    along = jnp.einsum("tsc,tc->ts", tangent, val_pull, precision=lax.Precision.HIGHEST)
    val_first = lax.axis_index("fsdp") * val_members
    val_local = lax.dynamic_slice_in_dim(val_skill, val_first, val_members)
    val_indicator = jnp.repeat(
        (val_local[:, None] == skill_ids[None, :]).astype(jnp.float32), VSEQ, axis=0
    )
    partial_transfer = step_size * jnp.dot(along.T, val_indicator, precision=lax.Precision.HIGHEST)
    transfer = lax.psum(partial_transfer, ("fsdp", "tp"))
    return (skill_grads, transfer)


def solution(mesh):
    placed = (
        P("fsdp", None),
        P("fsdp", "tp"),
        P("fsdp", "tp"),
        P("fsdp", "tp"),
        P(),
        P("fsdp", "tp"),
        P("fsdp", None),
        P("fsdp", "tp"),
        P("fsdp", "tp"),
        P("fsdp", "tp"),
        P(),
    )
    return jax.shard_map(
        on_device,
        mesh=mesh,
        in_specs=placed,
        out_specs=(P(None, "fsdp", "tp"), P()),
        check_vma=False,
    )
```

profile of v0, /device:TPU:1, one launch (start us, length us, event | category | flops | bytes accessed | tf_op | source)
XLA Modules:
  0.0 577.4 jit_solution(3521864218452400355)
XLA Ops:
  7.2 0.0 copy-start
  7.2 0.0 all-gather.3.cloned.1.call-start
  7.2 0.7 all-gather.3.cloned.1.call-update
  7.9 0.0 reduce-scatter.2.cloned.1.call-start
  8.0 3.6 copy.56
  11.5 2.0 convert_bitcast_fusion
  13.6 0.0 copy-start.6
  13.6 0.0 copy-start.4
  13.6 2.9 copy.57
  16.5 5.2 copy.28
  21.8 0.0 copy-done.6
  21.8 0.1 dynamic_slice.6
  21.9 0.1 fusion.66
  22.0 0.0 copy-done.4
  22.0 3.1 fusion.1
  25.0 0.0 copy-start.1
  25.0 3.2 copy-done.1
  28.2 1.9 fusion
  30.1 64.9 %all-gather.3.cloned.1.call-done = bf16[8192,128]{1,0:T(8,128)(2,1)} async-done(((bf16[256,128]{1,0:T(8,128)(2,1)}), bf16[8192,128]{1,0:T(8,128)(2,1)}) %all-gather.3.cloned.1.call-update) | async-done | bytes 2097168 | tf_op jit(solution)/shard_map/all_gather | solution.py:52
  95.0 10.8 %convolution_convert_fusion = bf16[1024,128]{1,0:T(8,128)(2,1)S(1)} fusion(bf16[1024,8192]{1,0:T(8,128)(2,1)} %param.11, bf16[8192,128]{1,0:T(8,128)(2,1)} %all-gather.3.cloned.1.call-done), kind=kOutput, calls=%fused_computation.35 | convolution fusion | flops 2147614720 | bytes 19136512 | tf_op jit(solution)/shard_map/dot_general | solution.py:53
  105.9 9.5 %fusion.42 = bf16[4,256,1,128]{1,3,0,2:T(8,128)(2,1)S(1)} fusion(f32[4,8,256]{2,1,0:T(8,128)S(1)} %fusion, f32[4,8,256]{2,1,0:T(8,128)S(1)} %get-tuple-element.6, f32[4,256,256,8]{2,1,3,0:T(8,128)} %copy-done.1, pred[256,256]{0,1:T(8,128)(4,1)S(1)} %iota_compare_fusion, f32[4,256,1,8,128]{1,4,3,0,2:T(8,128)} %copy.28, bf16[4,256,128,1]{2,1,3,0:T(8,128)(2,1)S(1)} %bitcast.216), kind=kOutput, calls=%fused_computation.38 | convolution fusion | flops 1097990144 | bytes 13238272 | tf_op jit(solution)/shard_map/bgrqk,bqgrh->bkgh/dot_general | solution.py:66
  115.4 4.9 convolution_bitcast_fusion
  120.3 4.9 convolution_bitcast_fusion.1
  125.2 4.9 convolution_bitcast_fusion.2
  130.1 4.8 convolution_bitcast_fusion.3
  134.9 5.6 copy.33
  140.5 5.6 copy.32
  146.1 5.6 copy.31
  151.6 5.6 copy.30
  157.2 12.5 %multiply_add_fusion = f32[8192,4,128]{2,0,1:T(8,128)} fusion(f32[8192,128]{1,0:T(8,128)} %copy.33, f32[4]{0:T(128)S(1)} %get-tuple-element.3, f32[8192,128]{1,0:T(8,128)} %copy.32, f32[4]{0:T(128)S(1)} %get-tuple-element.4, f32[8192,128]{1,0:T(8,128)} %copy.31, f32[4]{0:T(128)S(1)} %get-tuple-element.5, f32[8192,128]{1,0:T(8,128)} %copy.30, ...), kind=kLoop, calls=%fused_computation | loop fusion | flops 29360128 | bytes 33554496 | tf_op jit(solution)/shard_map/add | solution.py:83
  169.8 0.0 copy-start.5
  169.8 0.0 reduce-scatter.2.cloned.1.call-update
  169.8 0.0 all-gather.5.cloned.1.call-start
  169.9 212.2 %reduce-scatter.2.cloned.1.call-done = f32[256,4,128]{2,0,1:T(8,128)} async-done(((f32[8192,4,128]{2,0,1:T(8,128)}), f32[256,4,128]{2,0,1:T(8,128)}) %reduce-scatter.2.cloned.1.call-update) | async-done | bytes 524304 | tf_op jit(solution)/shard_map/reduce_scatter | solution.py:84
  382.1 1.8 convert_bitcast_fusion.1
  383.9 0.0 all-gather.5.cloned.1.call-update
  383.9 0.0 copy-done.2
  383.9 0.1 copy.36
  384.1 0.6 dynamic_slice.7
  384.7 0.6 compare_convert_fusion
  385.3 0.2 fusion.72
  385.6 0.1 fusion.59
  385.7 3.5 fusion.33
  389.2 1.5 convolution_bitcast_fusion.5
  390.7 99.5 %all-gather.5.cloned.1.call-done = bf16[4,8192,128]{2,1,0:T(8,128)(2,1)} async-done(((bf16[4,256,128]{2,1,0:T(8,128)(2,1)}), bf16[4,8192,128]{2,1,0:T(8,128)(2,1)}) %all-gather.5.cloned.1.call-update) | async-done | bytes 8388624 | tf_op jit(solution)/shard_map/all_gather | solution.py:105
  490.2 5.8 fusion.55
  495.9 0.2 convolution_multiply_fusion.1
  496.1 74.7 %psum.7 = f32[4,4]{1,0:T(4,128)} all-reduce(f32[4,4]{1,0:T(4,128)S(1)} %convolution_multiply_fusion.1), channel_id=1, replica_groups=mesh['fsdp'=32,'tp'=8] {'fsdp','tp'}, use_global_device_ids=true, to_apply=%region_5.6 | all-reduce | flops 16 | bytes 128 | tf_op jit(solution)/shard_map/psum | solution.py:115
  (10 shorter events, 0.1 us)
Async XLA Ops:
  7.2 378.5 %copy-start = (bf16[128,8192]{1,0:T(8,128)(2,1)S(1)}, bf16[128,8192]{1,0:T(8,128)(2,1)}, u32[]{:S(2)}) copy-start(bf16[128,8192]{1,0:T(8,128)(2,1)} %param.17) | copy-start | bytes 6291460
  7.2 87.8 %all-gather.3.cloned.1.call-start = ((), (), s32[]{:S(2)}) async-start(), calls=%async_computation.1 | async-start | bytes 2162688 | tf_op jit(solution)/shard_map/all_gather | solution.py:52
  7.9 374.2 %reduce-scatter.2.cloned.1.call-start = ((), (), s32[]{:S(2)}) async-start(), calls=%async_computation.2 | async-start | bytes 17301504 | tf_op jit(solution)/shard_map/reduce_scatter | solution.py:84
  13.6 8.2 %copy-start.6 = (s32[128]{0:T(128)S(1)}, s32[128]{0:T(128)}, u32[]{:S(2)}) copy-start(s32[128]{0:T(128)} %param.15) | copy-start | bytes 1540
  13.6 8.4 %copy-start.4 = (bf16[1024,128]{1,0:T(8,128)(2,1)S(1)}, bf16[1024,128]{1,0:T(8,128)(2,1)}, u32[]{:S(2)}) copy-start(bf16[1024,128]{1,0:T(8,128)(2,1)} %param.13) | copy-start | bytes 786436
  25.0 3.2 copy-start.1
  169.8 214.1 %copy-start.2 = (bf16[128,1024]{1,0:T(8,128)(2,1)S(1)}, bf16[128,1024]{1,0:T(8,128)(2,1)}, u32[]{:S(2)}) copy-start(bf16[128,1024]{1,0:T(8,128)(2,1)} %param.20) | copy-start | bytes 786436
  169.8 214.3 %copy-start.7 = (s32[32]{0:T(128)S(1)}, s32[32]{0:T(128)}, u32[]{:S(2)}) copy-start(s32[32]{0:T(128)} %param.21) | copy-start | bytes 388
  169.8 215.5 %copy-start.3 = (bf16[128,1024]{1,0:T(8,128)(2,1)S(1)}, bf16[128,1024]{1,0:T(8,128)(2,1)}, u32[]{:S(2)}) copy-start(bf16[128,1024]{1,0:T(8,128)(2,1)} %param.18) | copy-start | bytes 786436
  169.8 215.6 %copy-start.5 = (bf16[128,128]{1,0:T(8,128)(2,1)S(1)}, bf16[128,128]{1,0:T(8,128)(2,1)}, u32[]{:S(2)}) copy-start(bf16[128,128]{1,0:T(8,128)(2,1)} %param.19) | copy-start | bytes 98308
  169.8 320.4 %all-gather.5.cloned.1.call-start = ((), (), s32[]{:S(2)}) async-start(), calls=%async_computation.3 | async-start | bytes 8650752 | tf_op jit(solution)/shard_map/all_gather | solution.py:105
Sparse Core Ops, SparseCore 0:
  10.8 84.1 all-gather.2
  169.9 212.1 reduce-scatter.1
  385.9 104.2 all-gather.4
where the time goes:
time: 578 us; the launch traced here: 577 us
  waiting for transfers between devices  377 us (65%)
  blocking collectives  74.7 us (13%)
  matrix products  54.1 us (9%)
  local copies, waits for them, and re-layouts  38.1 us (7%)
  other arithmetic  19.1 us (3%)
  between operations  13.9 us (2%)
    reduce_scatter x1, waiting for transfers between devices, on_device(): shares = lax.psum_scatter(running, 'fsdp', scatter_dimension=0, tiled=True)  212 us
    all_gather x1, waiting for transfers between devices, on_device(): lax.all_gather(skill_grads, 'fsdp', axis=1, tiled=True)  99.5 us
    psum x1, blocking collectives, on_device(): transfer = lax.psum(partial_transfer, ('fsdp', 'tp'))  74.7 us
    all_gather x1, waiting for transfers between devices, on_device(): shard_rows = lax.all_gather(value_weight, 'fsdp', axis=0, tiled=True)  64.9 us
    dot_general x4, local copies, waits for them, and re-layouts, on_device(): jnp.dot(train_x[sequence * SEQ:(sequence + 1) * SEQ].T, grad_rows[sequenc...  22.3 us
    dot_general x4, matrix products, on_device(): jnp.dot(train_x[sequence * SEQ:(sequence + 1) * SEQ].T, grad_rows[sequenc...  19.5 us
    add x1, other arithmetic, on_device(): running + local_indicator[sequence][None, :, None] * product[:, None, :]  12.5 us
  transfers between devices with their start and end apart: 3, of which 3 were waited for; matrix products, arithmetic and copies ran while one was open for 4% of the time, Pallas kernels for 0%

commit v1 on v0

--- a/solution.py
+++ b/solution.py
@@ -112,7 +112,8 @@
         (val_local[:, None] == skill_ids[None, :]).astype(jnp.float32), VSEQ, axis=0
     )
     partial_transfer = step_size * jnp.dot(along.T, val_indicator, precision=lax.Precision.HIGHEST)
-    transfer = lax.psum(partial_transfer, ("fsdp", "tp"))
+    pieces = lax.all_gather(partial_transfer, ("fsdp", "tp"), axis=0, tiled=False)
+    transfer = pieces.sum(axis=0)
     return (skill_grads, transfer)
 
 

time: 578 us -> 1100 us (1.90); the launches traced: 577 us -> 1090 us
  blocking collectives: 74.7 us -> 611 us
  local copies, waits for them, and re-layouts: 38.1 us -> 16.6 us
    all_gather x0 -> x1, blocking collectives: none -> 611 us  [on_device(): lax.all_gather(partial_transfer, ('fsdp', 'tp'), axis=0, tiled=False)]
    psum x1 -> x0, blocking collectives: 74.7 us -> none  [on_device(): transfer = lax.psum(partial_transfer, ('fsdp', 'tp'))]
    dot_general x4 -> x0, local copies, waits for them, and re-layouts: 22.3 us -> none  [on_device(): jnp.dot(train_x[sequence * SEQ:(sequence + 1) * SEQ].T, grad_rows[sequenc...]
  transfers between devices with their start and end apart: 3 -> 3, of which waited for: 3 -> 3; matrix products, arithmetic and copies ran while one was open for 4% -> 3% of each run, Pallas kernels for 0% -> 0%
where the time goes in v1:
time: 1100 us; the launch traced here: 1090 us
  blocking collectives  611 us (56%)
  waiting for transfers between devices  382 us (35%)
  matrix products  47 us (4%)
  local copies, waits for them, and re-layouts  16.6 us (2%)
  other arithmetic  14.8 us (1%)
  between operations  13.9 us (1%)
    all_gather x1, blocking collectives, on_device(): lax.all_gather(partial_transfer, ('fsdp', 'tp'), axis=0, tiled=False)  611 us
    reduce_scatter x1, waiting for transfers between devices, on_device(): shares = lax.psum_scatter(running, 'fsdp', scatter_dimension=0, tiled=True)  213 us
    all_gather x1, waiting for transfers between devices, on_device(): lax.all_gather(skill_grads, 'fsdp', axis=1, tiled=True)  104 us
    all_gather x1, waiting for transfers between devices, on_device(): shard_rows = lax.all_gather(value_weight, 'fsdp', axis=0, tiled=True)  64.9 us
  transfers between devices with their start and end apart: 3, of which 3 were waited for; matrix products, arithmetic and copies ran while one was open for 3% of the time, Pallas kernels for 0%

profile of v1, /device:TPU:1, one launch (start us, length us, event | category | flops | bytes accessed | tf_op | source)
XLA Modules:
  0.0 1085.5 jit_solution(17230255528998577464)
XLA Ops:
  7.2 0.0 copy-start
  7.2 0.0 all-gather.5.cloned.1.call-start
  7.2 0.7 all-gather.5.cloned.1.call-update
  7.9 0.0 reduce-scatter.2.cloned.1.call-start
  8.0 3.6 copy.69
  11.5 2.0 convert_bitcast_fusion
  13.6 0.0 copy-start.6
  13.6 0.0 copy-start.4
  13.6 2.9 copy.70
  16.5 5.2 copy.41
  21.8 0.0 copy-done.6
  21.8 0.1 dynamic_slice.6
  21.9 0.1 fusion.67
  22.0 0.0 copy-done.4
  22.0 3.1 fusion.1
  25.0 0.0 copy-start.1
  25.0 3.2 copy-done.1
  28.2 1.9 fusion
  30.1 64.9 %all-gather.5.cloned.1.call-done = bf16[8192,128]{1,0:T(8,128)(2,1)} async-done(((bf16[256,128]{1,0:T(8,128)(2,1)}), bf16[8192,128]{1,0:T(8,128)(2,1)}) %all-gather.5.cloned.1.call-update) | async-done | bytes 2097168 | tf_op jit(solution)/shard_map/all_gather | solution.py:52
  95.0 10.8 convolution_convert_fusion
  105.9 9.5 fusion.42
  115.4 2.9 convolution_bitcast_fusion
  118.3 2.9 convolution_bitcast_fusion.1
  121.3 2.9 convolution_bitcast_fusion.2
  124.2 2.9 convolution_bitcast_fusion.3
  127.1 7.4 multiply_add_fusion
  134.5 0.0 reduce-scatter.2.cloned.1.call-update
  134.6 0.0 all-gather.7.cloned.1.call-start
  134.6 212.7 %reduce-scatter.2.cloned.1.call-done = f32[256,4,128]{0,2,1:T(8,128)} async-done(((f32[8192,4,128]{0,2,1:T(8,128)}), f32[256,4,128]{0,2,1:T(8,128)}) %reduce-scatter.2.cloned.1.call-update) | async-done | bytes 524304 | tf_op jit(solution)/shard_map/reduce_scatter | solution.py:84
  347.4 1.8 convert_bitcast_fusion.1
  349.1 0.0 all-gather.7.cloned.1.call-update
  349.2 0.0 copy-done.3
  349.2 0.1 copy.46
  349.3 0.0 copy-done.7
  349.3 0.6 dynamic_slice.7
  349.9 0.6 compare_convert_fusion
  350.6 0.0 copy-done.5
  350.6 1.2 fusion.73
  351.8 0.1 fusion.60
  351.9 3.4 fusion.33
  355.3 1.5 convolution_bitcast_fusion.5
  356.8 0.0 copy-done.2
  356.8 0.8 copy.48
  357.6 103.9 %all-gather.7.cloned.1.call-done = bf16[4,8192,128]{1,2,0:T(8,128)(2,1)} async-done(((bf16[4,256,128]{1,2,0:T(8,128)(2,1)}), bf16[4,8192,128]{1,2,0:T(8,128)(2,1)}) %all-gather.7.cloned.1.call-update) | async-done | bytes 8388624 | tf_op jit(solution)/shard_map/all_gather | solution.py:105
  461.5 5.7 fusion.55
  467.3 0.2 fusion.59
  467.4 610.7 %all-gather.1 = f32[256,4,4]{2,1,0:T(4,128)S(1)} all-gather(f32[1,4,4]{2,1,0:T(4,128)S(1)} %fusion.59), channel_id=2, replica_groups=mesh['fsdp'=32,'tp'=8] {'fsdp','tp'}, dimensions={0}, use_global_device_ids=true | all-gather | bytes 16448 | tf_op jit(solution)/shard_map/all_gather | solution.py:115
  1078.1 0.9 reduce_sum.29
  (8 shorter events, 0.1 us)
Async XLA Ops:
  7.2 344.7 %copy-start = (bf16[128,8192]{1,0:T(8,128)(2,1)S(1)}, bf16[128,8192]{1,0:T(8,128)(2,1)}, u32[]{:S(2)}) copy-start(bf16[128,8192]{1,0:T(8,128)(2,1)} %param.17) | copy-start | bytes 6291460
  7.2 87.8 %all-gather.5.cloned.1.call-start = ((), (), s32[]{:S(2)}) async-start(), calls=%async_computation.1 | async-start | bytes 2162688 | tf_op jit(solution)/shard_map/all_gather | solution.py:52
  7.9 339.4 %reduce-scatter.2.cloned.1.call-start = ((), (), s32[]{:S(2)}) async-start(), calls=%async_computation.2 | async-start | bytes 17301504 | tf_op jit(solution)/shard_map/reduce_scatter | solution.py:84
  13.6 8.2 copy-start.6
  13.6 8.4 copy-start.4
  25.0 3.2 copy-start.1
  134.5 214.6 %copy-start.3 = (bf16[128,1024]{1,0:T(8,128)(2,1)S(1)}, bf16[128,1024]{1,0:T(8,128)(2,1)}, u32[]{:S(2)}) copy-start(bf16[128,1024]{1,0:T(8,128)(2,1)} %param.20) | copy-start | bytes 786436
  134.5 214.8 %copy-start.7 = (s32[32]{0:T(128)S(1)}, s32[32]{0:T(128)}, u32[]{:S(2)}) copy-start(s32[32]{0:T(128)} %param.21) | copy-start | bytes 388
  134.5 216.1 %copy-start.5 = (bf16[128,128]{1,0:T(8,128)(2,1)S(1)}, bf16[128,128]{1,0:T(8,128)(2,1)}, u32[]{:S(2)}) copy-start(bf16[128,128]{1,0:T(8,128)(2,1)} %param.19) | copy-start | bytes 98308
  134.6 327.0 %all-gather.7.cloned.1.call-start = ((), (), s32[]{:S(2)}) async-start(), calls=%async_computation.3 | async-start | bytes 8650752 | tf_op jit(solution)/shard_map/all_gather | solution.py:105
  349.1 7.6 copy-start.2
Sparse Core Ops, SparseCore 0:
  10.8 84.1 all-gather.4
  134.7 212.6 reduce-scatter.1
  350.2 111.2 all-gather.6
